TPU v7x, 512 devices: a whole 4x8x8 slice. The times are simulated.
512 devices in a mesh: dp: 64 (over x, z, core), tensor: 8 (over y).
Axes of the slice: x: 4, y: 8, z: 8, core: 2. Of those that a mesh axis runs over, the one named last changes fastest.
Arguments:
- prompt_keys: bfloat16 [4096, 1024], P('dp', 'tensor'), may hold values from -6 to 6
- prompt_values: bfloat16 [4096, 1024], P('dp', 'tensor'), may hold values from -6 to 6
- key_weight: bfloat16 [5120, 1024], P('dp', 'tensor'), may hold values from -0.078125 to 0.078125
- value_weight: bfloat16 [5120, 1024], P('dp', 'tensor'), may hold values from -0.078125 to 0.078125
- resp_query: bfloat16 [8192, 8192], P('dp', 'tensor'), may hold values from -6 to 6
- resp_keys: bfloat16 [8192, 1024], P('dp', 'tensor'), may hold values from -6 to 6
- resp_values: bfloat16 [8192, 1024], P('dp', 'tensor'), may hold values from -6 to 6
- resp_grad: bfloat16 [8192, 8192], P('dp', 'tensor'), may hold values from -48 to 48
- resp_lse: float32 [64, 8192], P('tensor', 'dp'), as said below
- resp_delta: float32 [64, 8192], P('tensor', 'dp'), may hold values from -24 to 24
- resp_prompt: int32 [1024], replicated, may hold values from 0 to 63, as said below
- resp_lengths: int32 [1024], P('dp'), may hold values from 1 to 8, 5120 in all
Outputs:
- d_query: bfloat16 [8192, 8192], P('dp', 'tensor')
- d_resp_keys: bfloat16 [8192, 1024], P('dp', 'tensor')
- d_resp_values: bfloat16 [8192, 1024], P('dp', 'tensor')
- d_prompt_input: bfloat16 [4096, 5120], P('dp', 'tensor')
Inputs may be any that keep to these rules, and one draw needn't show every extreme that they name: `resp_prompt`: response r sits on index r // 16 of dp, in slot r % 16, and prompt p on index p. For each slot number s, the responses in slot s of all indices of dp name every prompt exactly once; so each prompt is named by exactly 16 responses, and the 16 responses of one index of dp name 16 different prompts. `resp_lse`: within 0.5 below and 1.5 above log(72).
All inputs are finite; a program needn't handle non-finite values. No bound on the sum of `resp_lengths` on one device may be relied on, other than what follows from the above.
Results may differ from a plain program's by a relative error of at most 0.006.
Values may be sent and summed in bfloat16 or wider, within the bound.
A program may use at most 64 MiB of HBM per device.

v0:
```python
import jax
import jax.numpy as jnp
from jax import lax
from jax.sharding import PartitionSpec as P

QH = 64
KVH = 8
HD = 128


def attend_back(query, grad_live, log_norm, row_delta, key_rows, value_rows, key_mask):
    scaling = query.shape[-1] ** (-0.5)
    scores = (
        jnp.einsum("crlgqd,cmgd->crlgqm", query, key_rows, preferred_element_type=jnp.float32)
        * scaling
    )
    probs = jnp.exp(scores - log_norm[..., None])
    if key_mask is not None:
        probs = jnp.where(key_mask[:, None, None, :], probs, jnp.float32(0.0))
    probs_low = probs.astype(jnp.bfloat16)
    dprob = jnp.einsum(
        "crlgqd,cmgd->crlgqm", grad_live, value_rows, preferred_element_type=jnp.float32
    )
    dscore = (probs * (dprob - row_delta[..., None])).astype(jnp.bfloat16)
    grad_values = jnp.einsum(
        "crlgqm,crlgqd->cmgd", probs_low, grad_live, preferred_element_type=jnp.float32
    )
    grad_keys = (
        jnp.einsum("crlgqm,crlgqd->cmgd", dscore, query, preferred_element_type=jnp.float32)
        * scaling
    )
    grad_query = (
        jnp.einsum("crlgqm,cmgd->crlgqd", dscore, key_rows, preferred_element_type=jnp.float32)
        * scaling
    )
    return (grad_query, grad_keys, grad_values)


def prefix_scan(items, own_keys, own_values, group_size):
    count = items[0].shape[0]
    blocks = tuple(
        (
            part_array.reshape((count // group_size, group_size) + part_array.shape[1:])
            for part_array in items
        )
    )
    kv_local = own_keys.shape[2]
    head_size = own_keys.shape[3]

    def one_block(carry, block):
        got_query, got_grad, got_norm, got_delta = block
        rows_n, rows_l = (got_query.shape[0], got_query.shape[1])
        shaped_query = got_query.reshape(1, rows_n, rows_l, kv_local, -1, head_size)
        shaped_grad = got_grad.reshape(1, rows_n, rows_l, kv_local, -1, head_size)
        grad_query, grad_keys, grad_values = attend_back(
            shaped_query, shaped_grad, got_norm[None], got_delta[None], own_keys, own_values, None
        )
        return (
            (carry[0] + grad_keys, carry[1] + grad_values),
            grad_query.reshape(rows_n, rows_l, -1),
        )

    start_sums = (jnp.zeros(own_keys.shape, jnp.float32), jnp.zeros(own_keys.shape, jnp.float32))
    (key_sum, value_sum), block_dq = lax.scan(one_block, start_sums, blocks)
    return (key_sum, value_sum, block_dq.reshape((count,) + block_dq.shape[2:]))


def contract(left, right):
    return lax.dot_general(
        left, right, (((1,), (1,)), ((), ())), preferred_element_type=jnp.float32
    )


def body(
    prompt_keys,
    prompt_values,
    key_weight,
    value_weight,
    resp_query,
    resp_keys,
    resp_values,
    resp_grad,
    resp_lse,
    resp_delta,
    resp_prompt,
    resp_lengths,
):
    dev_count = lax.axis_size("dp")
    my_index = lax.axis_index("dp")
    group_heads = QH // KVH
    kv_local = resp_keys.shape[1] // HD
    slots = resp_lengths.shape[0]
    resp_len = resp_query.shape[0] // slots
    prompt_len = prompt_keys.shape[0]
    feat_width = resp_query.shape[1]
    zero_low = jnp.zeros((), jnp.bfloat16)
    shaped = (slots, resp_len, kv_local, group_heads, HD)
    valid = jnp.arange(resp_len)[None, :] < resp_lengths[:, None]
    query = resp_query.reshape(shaped)
    grad_live = jnp.where(valid[:, :, None, None, None], resp_grad.reshape(shaped), zero_low)
    log_norm = resp_lse.reshape(kv_local, group_heads, slots, resp_len).transpose(2, 3, 0, 1)
    delta_all = resp_delta.reshape(kv_local, group_heads, slots, resp_len).transpose(2, 3, 0, 1)
    delta_live = jnp.where(valid[:, :, None, None], delta_all, jnp.float32(0.0))
    placed = resp_prompt.reshape(dev_count, slots)
    my_prompts = lax.dynamic_slice_in_dim(placed, my_index, 1, 0)[0]
    flat_query = resp_query.reshape(slots, resp_len, feat_width)
    flat_grad = grad_live.reshape(slots, resp_len, feat_width)
    causal = jnp.arange(resp_len)[:, None] >= jnp.arange(resp_len)[None, :]
    key_local = resp_keys.reshape(slots, resp_len, kv_local, HD)
    value_local = resp_values.reshape(slots, resp_len, kv_local, HD)
    local_dq, local_dk, local_dv = attend_back(
        query[:, None],
        grad_live[:, None],
        log_norm[:, None],
        delta_live[:, None],
        key_local,
        value_local,
        causal,
    )
    d_resp_keys = local_dk.astype(jnp.bfloat16).reshape(slots * resp_len, kv_local * HD)
    d_resp_values = local_dv.astype(jnp.bfloat16).reshape(slots * resp_len, kv_local * HD)
    own_keys = prompt_keys.reshape(1, prompt_len, kv_local, HD)
    own_values = prompt_values.reshape(1, prompt_len, kv_local, HD)
    match = my_prompts[None, :] == jnp.arange(dev_count)[:, None]
    present = jnp.any(match, axis=1)
    dest_slot = jnp.sum(jnp.where(match, jnp.arange(slots)[None, :], 0), axis=1)
    send_query = jnp.where(
        present[:, None, None], jnp.take(flat_query, dest_slot, axis=0), zero_low
    )
    send_grad = jnp.where(present[:, None, None], jnp.take(flat_grad, dest_slot, axis=0), zero_low)
    send_norm = jnp.where(
        present[:, None, None, None], jnp.take(log_norm, dest_slot, axis=0), jnp.float32(0.0)
    )
    send_delta = jnp.where(
        present[:, None, None, None], jnp.take(delta_live, dest_slot, axis=0), jnp.float32(0.0)
    )
    send_query, send_grad, send_norm, send_delta = (send_query, send_grad, send_norm, send_delta)
    got_query, got_grad = (
        lax.all_to_all(send_query, "dp", split_axis=0, concat_axis=0, tiled=True),
        lax.all_to_all(send_grad, "dp", split_axis=0, concat_axis=0, tiled=True),
    )
    got_norm, got_delta = (
        lax.all_to_all(send_norm, "dp", split_axis=0, concat_axis=0, tiled=True),
        lax.all_to_all(send_delta, "dp", split_axis=0, concat_axis=0, tiled=True),
    )
    key_sum, value_sum, block_dq = prefix_scan(
        (got_query, got_grad, got_norm, got_delta), own_keys, own_values, slots
    )
    prefix_dq = block_dq.astype(jnp.bfloat16)
    returned = lax.all_to_all(prefix_dq, "dp", split_axis=0, concat_axis=0, tiled=True)
    mine = jnp.take(returned, my_prompts, axis=0)
    d_query = (local_dq.reshape(slots, resp_len, feat_width) + mine.astype(jnp.float32)).astype(
        jnp.bfloat16
    )
    d_query = d_query.reshape(slots * resp_len, feat_width)
    dk_low = key_sum.reshape(prompt_len, kv_local * HD).astype(jnp.bfloat16)
    dv_low = value_sum.reshape(prompt_len, kv_local * HD).astype(jnp.bfloat16)
    stacked = jnp.stack((key_weight, value_weight))
    piece = lax.all_gather(stacked, "dp", axis=1, tiled=True)
    partial_sum = contract(dk_low, piece[0]) + contract(dv_low, piece[1])
    summed = lax.psum_scatter(partial_sum, "tensor", scatter_dimension=1, tiled=True)
    d_prompt_input = summed.astype(jnp.bfloat16)
    return (d_query, d_resp_keys, d_resp_values, d_prompt_input)


def solution(mesh):
    placed = (
        P("dp", "tensor"),
        P("dp", "tensor"),
        P("dp", "tensor"),
        P("dp", "tensor"),
        P("dp", "tensor"),
        P("dp", "tensor"),
        P("dp", "tensor"),
        P("dp", "tensor"),
        P("tensor", "dp"),
        P("tensor", "dp"),
        P(),
        P("dp"),
    )
    return jax.shard_map(
        body,
        mesh=mesh,
        in_specs=placed,
        out_specs=(P("dp", "tensor"), P("dp", "tensor"), P("dp", "tensor"), P("dp", "tensor")),
        check_vma=False,
    )
```

profile of v0, /device:TPU:2, one launch (start us, length us, event | category | flops | bytes accessed | tf_op | source)
XLA Modules:
  0.0 240.0 jit_solution(2691822412907780129)
XLA Ops:
  7.2 0.8 reshape.275
  8.6 0.8 copy.93
  12.3 1.0 fusion.39
  13.3 13.9 %all-to-all-start.1 = ((f32[64,8,1,8]{3,1,2,0:T(8,128)}), f32[64,8,1,8]{3,1,2,0:T(8,128)S(1)}, u32[]{:S(2)}, u32[]{:S(2)}) async-start(f32[64,8,1,8]{3,1,2,0:T(8,128)} %get-tuple-element.163), calls=%async_computation.1 | async-start | bytes 524288 | tf_op jit(solution)/shard_map/all_to_all | solution.py:143
  28.5 10.2 %all-to-all-done.1 = f32[64,8,1,8]{3,1,2,0:T(8,128)S(1)} async-done(((f32[64,8,1,8]{3,1,2,0:T(8,128)}), f32[64,8,1,8]{3,1,2,0:T(8,128)S(1)}, u32[]{:S(2)}, u32[]{:S(2)}) %all-to-all-start.1) | async-done | bytes 16416 | tf_op jit(solution)/shard_map/all_to_all | solution.py:143
  39.4 6.7 %all-to-all-start.3 = ((f32[64,8,1,8]{3,1,2,0:T(8,128)}), f32[64,8,1,8]{3,1,2,0:T(8,128)}, u32[]{:S(2)}, u32[]{:S(2)}) async-start(f32[64,8,1,8]{3,1,2,0:T(8,128)} %get-tuple-element.162), calls=%async_computation.3 | async-start | bytes 524288 | tf_op jit(solution)/shard_map/all_to_all | solution.py:144
  46.1 1.3 select_select_fusion
  47.4 10.1 %all-to-all-done.3 = f32[64,8,1,8]{3,1,2,0:T(8,128)} async-done(((f32[64,8,1,8]{3,1,2,0:T(8,128)}), f32[64,8,1,8]{3,1,2,0:T(8,128)}, u32[]{:S(2)}, u32[]{:S(2)}) %all-to-all-start.3) | async-done | bytes 16416 | tf_op jit(solution)/shard_map/all_to_all | solution.py:144
  57.5 33.4 %all_to_all.25 = bf16[64,8,1024]{2,1,0:T(8,128)(2,1)S(1)} all-to-all(bf16[64,8,1024]{2,1,0:T(8,128)(2,1)S(1)} %get-tuple-element.165), channel_id=1, replica_groups=mesh['dp'=64,'tensor'=8] {'dp'}, dimensions={0} | all-to-all | bytes 2097152 | tf_op jit(solution)/shard_map/all_to_all | solution.py:139
  91.0 8.0 %all-to-all-start.2 = ((bf16[64,8,1024]{2,1,0:T(8,128)(2,1)}), bf16[64,8,1024]{2,1,0:T(8,128)(2,1)}, u32[]{:S(2)}, u32[]{:S(2)}) async-start(bf16[64,8,1024]{2,1,0:T(8,128)(2,1)} %get-tuple-element.164), calls=%async_computation.2 | async-start | bytes 2097152 | tf_op jit(solution)/shard_map/all_to_all | solution.py:140
  99.7 26.2 %all-to-all-done.2 = bf16[64,8,1024]{2,1,0:T(8,128)(2,1)} async-done(((bf16[64,8,1024]{2,1,0:T(8,128)(2,1)}), bf16[64,8,1024]{2,1,0:T(8,128)(2,1)}, u32[]{:S(2)}, u32[]{:S(2)}) %all-to-all-start.2) | async-done | bytes 1048608 | tf_op jit(solution)/shard_map/all_to_all | solution.py:140
  126.0 15.7 %while.15 = (s32[]{:T(128)}, f32[1,64,1,128]{3,1,2,0:T(8,128)S(1)}, f32[1,64,1,128]{3,1,2,0:T(8,128)S(1)}, bf16[4,16,8,1024]{3,2,1,0:T(8,128)(2,1)}, bf16[4,16,8...) while((s32[]{:T(128)}, f32[1,64,1,128]{3,1,2,0:T(8,128)S(1)}, ...), condition=%wide.region_3.6_spmd.clone, body=%wide.region_2.5_spmd.clone.sunk | while | flops 84582400 | bytes 4792468 | solution.py:64
  126.0 0.9 dynamic-slice_bitcast_fusion.6
  126.8 1.0 dynamic-slice_bitcast_fusion.7
  129.9 0.9 dynamic-slice_bitcast_fusion.6
  130.8 1.0 dynamic-slice_bitcast_fusion.7
  133.8 0.9 dynamic-slice_bitcast_fusion.6
  134.7 1.0 dynamic-slice_bitcast_fusion.7
  137.8 0.9 dynamic-slice_bitcast_fusion.6
  138.7 1.0 dynamic-slice_bitcast_fusion.7
  141.7 46.2 %all-gather.2.cloned.1.call-done = bf16[2,5120,128]{2,1,0:T(8,128)(2,1)} async-done(((bf16[2,80,128]{2,1,0:T(8,128)(2,1)}), bf16[2,5120,128]{2,1,0:T(8,128)(2,1)}) %all-gather.2.cloned.1.call-update) | async-done | bytes 2621456 | tf_op jit(solution)/shard_map/all_gather | solution.py:159
  187.9 2.0 fusion.19
  190.1 1.6 convolution_add_fusion
  191.8 7.6 %all-to-all-start.4 = ((bf16[64,8,1024]{2,1,0:T(8,128)(2,1)}), bf16[64,8,1024]{2,1,0:T(8,128)(2,1)S(1)}, u32[]{:S(2)}, u32[]{:S(2)}) async-start(bf16[64,8,1024]{2,1,0:T(8,128)(2,1)} %bitcast.41), calls=%async_computation.4 | async-start | bytes 2097152 | tf_op jit(solution)/shard_map/all_to_all | solution.py:150
  200.3 1.3 fusion.28
  201.6 1.3 fusion.30
  203.0 1.0 fusion.34
  204.0 1.0 fusion.35
  205.3 21.3 %all-to-all-done.4 = bf16[64,8,1024]{2,1,0:T(8,128)(2,1)S(1)} async-done(((bf16[64,8,1024]{2,1,0:T(8,128)(2,1)}), bf16[64,8,1024]{2,1,0:T(8,128)(2,1)S(1)}, u32[]{:S(2)}, u32[]{:S(2)}) %all-to-all-start.4) | async-done | bytes 1048608 | tf_op jit(solution)/shard_map/all_to_all | solution.py:150
  227.1 0.9 fusion.36
  228.0 3.5 %reduce-scatter.2.cloned.1.call-done = f32[64,640]{1,0:T(8,128)} async-done(((f32[64,5120]{1,0:T(8,128)}), f32[64,640]{1,0:T(8,128)}) %reduce-scatter.2.cloned.1.call-update) | async-done | bytes 163856 | tf_op jit(solution)/shard_map/reduce_scatter | solution.py:161
  231.6 1.6 convert_element_type.80
  (81 shorter events, 16.2 us)
Async XLA Ops:
  7.2 20.7 %copy-start = (bf16[128,1024]{1,0:T(8,128)(2,1)S(1)}, bf16[128,1024]{1,0:T(8,128)(2,1)}, u32[]{:S(2)}) copy-start(bf16[128,1024]{1,0:T(8,128)(2,1)} %param.22) | copy-start | bytes 786436
  8.0 0.6 copy-start.7
  11.0 16.2 %copy-start.2 = (bf16[128,1024]{1,0:T(8,128)(2,1)S(1)}, bf16[128,1024]{1,0:T(8,128)(2,1)}, u32[]{:S(2)}) copy-start(bf16[128,1024]{1,0:T(8,128)(2,1)} %param.25) | copy-start | bytes 786436
  13.3 25.4 %all-to-all-start.1 = ((f32[64,8,1,8]{3,1,2,0:T(8,128)}), f32[64,8,1,8]{3,1,2,0:T(8,128)S(1)}, u32[]{:S(2)}, u32[]{:S(2)}) async-start(f32[64,8,1,8]{3,1,2,0:T(8,128)} %get-tuple-element.163), calls=%async_computation.1 | async-start | bytes 524288 | tf_op jit(solution)/shard_map/all_to_all | solution.py:143
  38.7 0.7 copy-start.4
  39.4 18.1 %all-to-all-start.3 = ((f32[64,8,1,8]{3,1,2,0:T(8,128)}), f32[64,8,1,8]{3,1,2,0:T(8,128)}, u32[]{:S(2)}, u32[]{:S(2)}) async-start(f32[64,8,1,8]{3,1,2,0:T(8,128)} %get-tuple-element.162), calls=%async_computation.3 | async-start | bytes 524288 | tf_op jit(solution)/shard_map/all_to_all | solution.py:144
  90.9 8.0 %copy-start.10 = (bf16[80,128]{1,0:T(8,128)(2,1)S(1)}, bf16[80,128]{1,0:T(8,128)(2,1)}, u32[]{:S(2)}) copy-start(bf16[80,128]{1,0:T(8,128)(2,1)} %param.21) | copy-start | bytes 61444
  90.9 8.0 %copy-start.11 = (bf16[80,128]{1,0:T(8,128)(2,1)S(1)}, bf16[80,128]{1,0:T(8,128)(2,1)}, u32[]{:S(2)}) copy-start(bf16[80,128]{1,0:T(8,128)(2,1)} %param.20) | copy-start | bytes 61444
  90.9 35.0 %copy-start.5 = (bf16[64,128]{1,0:T(8,128)(2,1)S(1)}, bf16[64,128]{1,0:T(8,128)(2,1)}, u32[]{:S(2)}) copy-start(bf16[64,128]{1,0:T(8,128)(2,1)} %param.19) | copy-start | bytes 49156
  90.9 35.0 %copy-start.6 = (bf16[64,128]{1,0:T(8,128)(2,1)S(1)}, bf16[64,128]{1,0:T(8,128)(2,1)}, u32[]{:S(2)}) copy-start(bf16[64,128]{1,0:T(8,128)(2,1)} %param.18) | copy-start | bytes 49156
  91.0 35.0 %all-to-all-start.2 = ((bf16[64,8,1024]{2,1,0:T(8,128)(2,1)}), bf16[64,8,1024]{2,1,0:T(8,128)(2,1)}, u32[]{:S(2)}, u32[]{:S(2)}) async-start(bf16[64,8,1024]{2,1,0:T(8,128)(2,1)} %get-tuple-element.164), calls=%async_computation.2 | async-start | bytes 2097152 | tf_op jit(solution)/shard_map/all_to_all | solution.py:140
  98.9 89.0 %all-gather.2.cloned.1.call-start = ((), (), s32[]{:S(2)}) async-start(), calls=%async_computation.6 | async-start | bytes 2662400 | tf_op jit(solution)/shard_map/all_gather | solution.py:159
  99.7 131.9 %reduce-scatter.2.cloned.1.call-start = ((), (), s32[]{:S(2)}) async-start(), calls=%async_computation.7 | async-start | bytes 1474560 | tf_op jit(solution)/shard_map/reduce_scatter | solution.py:161
  187.9 2.1 copy-start.1
  191.8 8.6 %copy-start.9 = (bf16[128,128]{1,0:T(8,128)(2,1)S(1)}, bf16[128,128]{1,0:T(8,128)(2,1)}, u32[]{:S(2)}) copy-start(bf16[128,128]{1,0:T(8,128)(2,1)} %param.23) | copy-start | bytes 98308
  191.8 9.8 %copy-start.3 = (bf16[128,1024]{1,0:T(8,128)(2,1)S(1)}, bf16[128,1024]{1,0:T(8,128)(2,1)}, u32[]{:S(2)}) copy-start(bf16[128,1024]{1,0:T(8,128)(2,1)} %param.25) | copy-start | bytes 786436
  191.8 9.8 %copy-start.8 = (bf16[128,128]{1,0:T(8,128)(2,1)S(1)}, bf16[128,128]{1,0:T(8,128)(2,1)}, u32[]{:S(2)}) copy-start(bf16[128,128]{1,0:T(8,128)(2,1)} %param.24) | copy-start | bytes 98308
  191.8 34.8 %all-to-all-start.4 = ((bf16[64,8,1024]{2,1,0:T(8,128)(2,1)}), bf16[64,8,1024]{2,1,0:T(8,128)(2,1)S(1)}, u32[]{:S(2)}, u32[]{:S(2)}) async-start(bf16[64,8,1024]{2,1,0:T(8,128)(2,1)} %bitcast.41), calls=%async_computation.4 | async-start | bytes 2097152 | tf_op jit(solution)/shard_map/all_to_all | solution.py:150
Sparse Core Ops, SparseCore 0:
  103.6 84.2 all-gather.1
  191.9 39.6 reduce-scatter.1
where the time goes:
time: 241 us; the launch traced here: 240 us
  waiting for transfers between devices  118 us (49%)
  starting transfers between devices  36.2 us (15%)
  blocking collectives  33.4 us (14%)
  local copies, waits for them, and re-layouts  17.7 us (7%)
  between operations  14.3 us (6%)
  matrix products  13.3 us (6%)
  other arithmetic  7.21 us (3%)
    all_gather x1, waiting for transfers between devices, body(): piece = lax.all_gather(stacked, 'dp', axis=1, tiled=True)  46.2 us
    all_to_all x1, blocking collectives, body(): lax.all_to_all(send_query, 'dp', split_axis=0, concat_axis=0, tiled=True)  33.4 us
    all_to_all x1, waiting for transfers between devices, body(): lax.all_to_all(send_grad, 'dp', split_axis=0, concat_axis=0, tiled=True)  26.2 us
    all_to_all x1, waiting for transfers between devices, body(): lax.all_to_all(prefix_dq, 'dp', split_axis=0, concat_axis=0, tiled=True)  21.3 us
    all_to_all x1, starting transfers between devices, body(): lax.all_to_all(send_norm, 'dp', split_axis=0, concat_axis=0, tiled=True)  13.9 us
    all_to_all x1, waiting for transfers between devices, body(): lax.all_to_all(send_norm, 'dp', split_axis=0, concat_axis=0, tiled=True)  10.2 us
    all_to_all x1, waiting for transfers between devices, body(): lax.all_to_all(send_delta, 'dp', split_axis=0, concat_axis=0, tiled=True)  10.1 us
    all_to_all x1, starting transfers between devices, body(): lax.all_to_all(send_grad, 'dp', split_axis=0, concat_axis=0, tiled=True)  7.95 us
  transfers between devices with their start and end apart: 6, of which 6 were waited for; matrix products, arithmetic and copies ran while one was open for 11% of the time, Pallas kernels for 0%

commit v1 on v0

--- a/solution.py
+++ b/solution.py
@@ -156,7 +156,15 @@
     dk_low = key_sum.reshape(prompt_len, kv_local * HD).astype(jnp.bfloat16)
     dv_low = value_sum.reshape(prompt_len, kv_local * HD).astype(jnp.bfloat16)
     stacked = jnp.stack((key_weight, value_weight))
-    piece = lax.all_gather(stacked, "dp", axis=1, tiled=True)
+    piece = jnp.concatenate(
+        lax.all_to_all(
+            jnp.stack(lax.axis_size("dp") * [stacked], axis=0),
+            axis_name="dp",
+            concat_axis=0,
+            split_axis=0,
+        ),
+        axis=1,
+    )
     partial_sum = contract(dk_low, piece[0]) + contract(dv_low, piece[1])
     summed = lax.psum_scatter(partial_sum, "tensor", scatter_dimension=1, tiled=True)
     d_prompt_input = summed.astype(jnp.bfloat16)

time: 241 us -> 250 us (1.037)
  the two profiles are of different devices: /device:TPU:2 before, /device:TPU:4 now
where the time goes in v1:
time: 250 us; the launch traced here: 248 us
  waiting for transfers between devices  99.9 us (40%)
  starting transfers between devices  46.2 us (18%)
  blocking collectives  33 us (13%)
  matrix products  28.6 us (11%)
  local copies, waits for them, and re-layouts  18.9 us (8%)
  between operations  14.4 us (6%)
  other arithmetic  7.15 us (3%)
    all_to_all x1, blocking collectives, body(): lax.all_to_all(send_grad, 'dp', split_axis=0, concat_axis=0, tiled=True)  33 us
    all_to_all x1, waiting for transfers between devices, body(): lax.all_to_all(jnp.stack(lax.axis_size('dp') * [stacked], axis=0), axis_n...  28 us
    all_to_all x1, waiting for transfers between devices, body(): lax.all_to_all(send_query, 'dp', split_axis=0, concat_axis=0, tiled=True)  26.6 us
    all_to_all x1, waiting for transfers between devices, body(): lax.all_to_all(prefix_dq, 'dp', split_axis=0, concat_axis=0, tiled=True)  20.8 us
    all_to_all x1, starting transfers between devices, body(): lax.all_to_all(send_delta, 'dp', split_axis=0, concat_axis=0, tiled=True)  14.1 us
    all_to_all x1, waiting for transfers between devices, body(): lax.all_to_all(send_norm, 'dp', split_axis=0, concat_axis=0, tiled=True)  10.2 us
    all_to_all x1, waiting for transfers between devices, body(): lax.all_to_all(send_delta, 'dp', split_axis=0, concat_axis=0, tiled=True)  10.1 us
    all_to_all x1, starting transfers between devices, body(): lax.all_to_all(prefix_dq, 'dp', split_axis=0, concat_axis=0, tiled=True)  8.91 us
  transfers between devices with their start and end apart: 6, of which 6 were waited for; matrix products, arithmetic and copies ran while one was open for 17% of the time, Pallas kernels for 0%

profile of v1, /device:TPU:4, one launch (start us, length us, event | category | flops | bytes accessed | tf_op | source)
XLA Modules:
  0.0 248.2 jit_solution(15018884568402957486)
XLA Ops:
  13.5 14.1 %all-to-all-start.3 = ((f32[64,8,1,8]{3,1,2,0:T(8,128)}), f32[64,8,1,8]{3,1,2,0:T(8,128)}, u32[]{:S(2)}, u32[]{:S(2)}) async-start(f32[64,8,1,8]{3,1,2,0:T(8,128)} %get-tuple-element.164), calls=%async_computation.3 | async-start | bytes 524288 | tf_op jit(solution)/shard_map/all_to_all | solution.py:144
  29.0 10.1 %all-to-all-done.3 = f32[64,8,1,8]{3,1,2,0:T(8,128)} async-done(((f32[64,8,1,8]{3,1,2,0:T(8,128)}), f32[64,8,1,8]{3,1,2,0:T(8,128)}, u32[]{:S(2)}, u32[]{:S(2)}) %all-to-all-start.3) | async-done | bytes 16416 | tf_op jit(solution)/shard_map/all_to_all | solution.py:144
  39.1 6.7 %all-to-all-start.1 = ((f32[64,8,1,8]{3,1,2,0:T(8,128)}), f32[64,8,1,8]{3,1,2,0:T(8,128)}, u32[]{:S(2)}, u32[]{:S(2)}) async-start(f32[64,8,1,8]{3,1,2,0:T(8,128)} %get-tuple-element.165), calls=%async_computation.1 | async-start | bytes 524288 | tf_op jit(solution)/shard_map/all_to_all | solution.py:143
  45.7 1.3 select_select_fusion
  47.0 10.2 %all-to-all-done.1 = f32[64,8,1,8]{3,1,2,0:T(8,128)} async-done(((f32[64,8,1,8]{3,1,2,0:T(8,128)}), f32[64,8,1,8]{3,1,2,0:T(8,128)}, u32[]{:S(2)}, u32[]{:S(2)}) %all-to-all-start.1) | async-done | bytes 16416 | tf_op jit(solution)/shard_map/all_to_all | solution.py:143
  57.2 33.0 %all_to_all.30 = bf16[64,8,1024]{2,1,0:T(8,128)(2,1)} all-to-all(bf16[64,8,1024]{2,1,0:T(8,128)(2,1)S(1)} %get-tuple-element.166), channel_id=1, replica_groups=mesh['dp'=64,'tensor'=8] {'dp'}, dimensions={0} | all-to-all | bytes 2097152 | tf_op jit(solution)/shard_map/all_to_all | solution.py:140
  90.2 8.2 %all-to-all-start = ((bf16[64,8,1024]{2,1,0:T(8,128)(2,1)}), bf16[64,8,1024]{2,1,0:T(8,128)(2,1)S(1)}, u32[]{:S(2)}, u32[]{:S(2)}) async-start(bf16[64,8,1024]{2,1,0:T(8,128)(2,1)} %get-tuple-element.167), calls=%async_computation | async-start | bytes 2097152 | tf_op jit(solution)/shard_map/all_to_all | solution.py:139
  98.5 26.6 %all-to-all-done = bf16[64,8,1024]{2,1,0:T(8,128)(2,1)S(1)} async-done(((bf16[64,8,1024]{2,1,0:T(8,128)(2,1)}), bf16[64,8,1024]{2,1,0:T(8,128)(2,1)S(1)}, u32[]{:S(2)}, u32[]{:S(2)}) %all-to-all-start) | async-done | bytes 1048608 | tf_op jit(solution)/shard_map/all_to_all | solution.py:139
  125.1 1.8 stack.11
  127.0 8.2 %all-to-all-start.5 = ((bf16[64,2,80,128]{3,2,1,0:T(8,128)(2,1)}), bf16[64,2,80,128]{3,2,1,0:T(8,128)(2,1)S(1)}, u32[]{:S(2)}, u32[]{:S(2)}) async-start(bf16[64,2,80,128]{3,2,1,0:T(8,128)(2,1)} %stack.11), calls=%async_computation.5 | async-start | bytes 5242880 | tf_op jit(solution)/shard_map/all_to_all | solution.py:160
  135.3 31.3 %while.15 = (s32[]{:T(128)}, f32[1,64,1,128]{3,1,2,0:T(8,128)}, f32[1,64,1,128]{3,1,2,0:T(8,128)}, bf16[4,16,8,1024]{3,2,1,0:T(8,128)(2,1)}, bf16[4,16,8,1024]{3...) while((s32[]{:T(128)}, f32[1,64,1,128]{3,1,2,0:T(8,128)}, ...), condition=%wide.region_3.6_spmd.clone, body=%wide.region_2.5_spmd.clone.sunk | while | flops 84582400 | bytes 4792468 | solution.py:64
  136.2 1.1 dynamic-slice_bitcast_fusion.7
  142.8 1.1 dynamic-slice_bitcast_fusion.7
  144.9 1.6 fusion.91
  146.7 1.6 fusion.90
  151.0 1.1 dynamic-slice_bitcast_fusion.7
  153.1 1.6 fusion.91
  154.9 1.6 fusion.90
  159.2 1.1 dynamic-slice_bitcast_fusion.7
  161.3 1.6 fusion.91
  163.1 1.6 fusion.90
  166.5 28.0 %all-to-all-done.5 = bf16[64,2,80,128]{3,2,1,0:T(8,128)(2,1)S(1)} async-done(((bf16[64,2,80,128]{3,2,1,0:T(8,128)(2,1)}), bf16[64,2,80,128]{3,2,1,0:T(8,128)(2,1)S(1)}, u32[]{:S(2)}, u32[]{:S(2)}) %all-to-all-start.5) | async-done | bytes 2621472 | tf_op jit(solution)/shard_map/all_to_all | solution.py:160
  194.7 1.3 fusion.51
  196.1 2.4 convolution_add_fusion
  198.5 8.9 %all-to-all-start.4 = ((bf16[64,8,1024]{2,1,0:T(8,128)(2,1)}), bf16[64,8,1024]{2,1,0:T(8,128)(2,1)S(1)}, u32[]{:S(2)}, u32[]{:S(2)}) async-start(bf16[64,8,1024]{2,1,0:T(8,128)(2,1)} %bitcast.41), calls=%async_computation.4 | async-start | bytes 2097152 | tf_op jit(solution)/shard_map/all_to_all | solution.py:150
  208.4 1.3 fusion.27
  209.7 1.3 fusion.29
  211.0 1.0 fusion.33
  212.0 1.0 fusion.34
  213.3 20.8 %all-to-all-done.4 = bf16[64,8,1024]{2,1,0:T(8,128)(2,1)S(1)} async-done(((bf16[64,8,1024]{2,1,0:T(8,128)(2,1)}), bf16[64,8,1024]{2,1,0:T(8,128)(2,1)S(1)}, u32[]{:S(2)}, u32[]{:S(2)}) %all-to-all-start.4) | async-done | bytes 1048608 | tf_op jit(solution)/shard_map/all_to_all | solution.py:150
  235.6 4.2 %reduce-scatter.2.cloned.1.call-done = f32[64,640]{1,0:T(8,128)} async-done(((f32[64,5120]{1,0:T(8,128)}), f32[64,640]{1,0:T(8,128)}) %reduce-scatter.2.cloned.1.call-update) | async-done | bytes 163856 | tf_op jit(solution)/shard_map/reduce_scatter | solution.py:169
  239.8 1.6 convert_element_type.80
  (84 shorter events, 27.6 us)
Async XLA Ops:
  7.2 21.2 %copy-start = (bf16[128,1024]{1,0:T(8,128)(2,1)S(1)}, bf16[128,1024]{1,0:T(8,128)(2,1)}, u32[]{:S(2)}) copy-start(bf16[128,1024]{1,0:T(8,128)(2,1)} %param.22) | copy-start | bytes 786436
  8.0 1.5 copy-start.7
  9.5 18.1 %copy-start.5 = (pred[16,8]{1,0:T(8,128)(4,1)}, pred[16,8]{1,0:T(8,128)(4,1)S(1)}, u32[]{:S(2)}) copy-start(pred[16,8]{1,0:T(8,128)(4,1)S(1)} %iota_compare_fusion.1) | copy-start | bytes 388
  11.2 16.4 %copy-start.2 = (bf16[128,1024]{1,0:T(8,128)(2,1)S(1)}, bf16[128,1024]{1,0:T(8,128)(2,1)}, u32[]{:S(2)}) copy-start(bf16[128,1024]{1,0:T(8,128)(2,1)} %param.25) | copy-start | bytes 786436
  13.5 25.6 %all-to-all-start.3 = ((f32[64,8,1,8]{3,1,2,0:T(8,128)}), f32[64,8,1,8]{3,1,2,0:T(8,128)}, u32[]{:S(2)}, u32[]{:S(2)}) async-start(f32[64,8,1,8]{3,1,2,0:T(8,128)} %get-tuple-element.164), calls=%async_computation.3 | async-start | bytes 524288 | tf_op jit(solution)/shard_map/all_to_all | solution.py:144
  39.1 18.1 %all-to-all-start.1 = ((f32[64,8,1,8]{3,1,2,0:T(8,128)}), f32[64,8,1,8]{3,1,2,0:T(8,128)}, u32[]{:S(2)}, u32[]{:S(2)}) async-start(f32[64,8,1,8]{3,1,2,0:T(8,128)} %get-tuple-element.165), calls=%async_computation.1 | async-start | bytes 524288 | tf_op jit(solution)/shard_map/all_to_all | solution.py:143
  90.2 8.3 %copy-start.10 = (bf16[80,128]{1,0:T(8,128)(2,1)S(1)}, bf16[80,128]{1,0:T(8,128)(2,1)}, u32[]{:S(2)}) copy-start(bf16[80,128]{1,0:T(8,128)(2,1)} %param.21) | copy-start | bytes 61444
  90.2 8.3 %copy-start.11 = (bf16[80,128]{1,0:T(8,128)(2,1)S(1)}, bf16[80,128]{1,0:T(8,128)(2,1)}, u32[]{:S(2)}) copy-start(bf16[80,128]{1,0:T(8,128)(2,1)} %param.20) | copy-start | bytes 61444
  90.2 34.9 %all-to-all-start = ((bf16[64,8,1024]{2,1,0:T(8,128)(2,1)}), bf16[64,8,1024]{2,1,0:T(8,128)(2,1)S(1)}, u32[]{:S(2)}, u32[]{:S(2)}) async-start(bf16[64,8,1024]{2,1,0:T(8,128)(2,1)} %get-tuple-element.167), calls=%async_computation | async-start | bytes 2097152 | tf_op jit(solution)/shard_map/all_to_all | solution.py:139
  125.1 1.9 copy-start.1
  127.0 8.3 %copy-start.4 = (bf16[64,128]{1,0:T(8,128)(2,1)S(1)}, bf16[64,128]{1,0:T(8,128)(2,1)}, u32[]{:S(2)}) copy-start(bf16[64,128]{1,0:T(8,128)(2,1)} %param.19) | copy-start | bytes 49156
  127.0 67.6 %all-to-all-start.5 = ((bf16[64,2,80,128]{3,2,1,0:T(8,128)(2,1)}), bf16[64,2,80,128]{3,2,1,0:T(8,128)(2,1)S(1)}, u32[]{:S(2)}, u32[]{:S(2)}) async-start(bf16[64,2,80,128]{3,2,1,0:T(8,128)(2,1)} %stack.11), calls=%async_computation.5 | async-start | bytes 5242880 | tf_op jit(solution)/shard_map/all_to_all | solution.py:160
  135.2 104.6 %reduce-scatter.2.cloned.1.call-start = ((), (), s32[]{:S(2)}) async-start(), calls=%async_computation.7 | async-start | bytes 1474560 | tf_op jit(solution)/shard_map/reduce_scatter | solution.py:169
  198.5 9.0 %copy-start.12 = (pred[16]{0:T(512)(128)(4,1)S(1)}, pred[16]{0:T(512)(128)(4,1)}, u32[]{:S(2)}) copy-start(pred[16]{0:T(512)(128)(4,1)} %get-tuple-element.156) | copy-start | bytes 52
  198.5 9.9 %copy-start.9 = (bf16[128,128]{1,0:T(8,128)(2,1)S(1)}, bf16[128,128]{1,0:T(8,128)(2,1)}, u32[]{:S(2)}) copy-start(bf16[128,128]{1,0:T(8,128)(2,1)} %param.23) | copy-start | bytes 98308
  198.5 11.1 %copy-start.3 = (bf16[128,1024]{1,0:T(8,128)(2,1)S(1)}, bf16[128,1024]{1,0:T(8,128)(2,1)}, u32[]{:S(2)}) copy-start(bf16[128,1024]{1,0:T(8,128)(2,1)} %param.25) | copy-start | bytes 786436
  198.5 11.1 %copy-start.6 = (pred[16,8]{1,0:T(8,128)(4,1)S(1)}, pred[16,8]{1,0:T(8,128)(4,1)}, u32[]{:S(2)}) copy-start(pred[16,8]{1,0:T(8,128)(4,1)} %copy-done.5) | copy-start | bytes 388
  198.5 11.1 %copy-start.8 = (bf16[128,128]{1,0:T(8,128)(2,1)S(1)}, bf16[128,128]{1,0:T(8,128)(2,1)}, u32[]{:S(2)}) copy-start(bf16[128,128]{1,0:T(8,128)(2,1)} %param.24) | copy-start | bytes 98308
  198.5 35.6 %all-to-all-start.4 = ((bf16[64,8,1024]{2,1,0:T(8,128)(2,1)}), bf16[64,8,1024]{2,1,0:T(8,128)(2,1)S(1)}, u32[]{:S(2)}, u32[]{:S(2)}) async-start(bf16[64,8,1024]{2,1,0:T(8,128)(2,1)} %bitcast.41), calls=%async_computation.4 | async-start | bytes 2097152 | tf_op jit(solution)/shard_map/all_to_all | solution.py:150
Sparse Core Ops, SparseCore 0:
  198.6 41.1 reduce-scatter.1
